TPU v7x, 32 devices: a whole 2x2x4 slice. The times are simulated.
32 devices in a mesh: grp: 2 (over y), tile: 16 (over z, x, core).
Axes of the slice: x: 2, y: 2, z: 4, core: 2. Of those that a mesh axis runs over, the one named last changes fastest.
Arguments:
- sensitivity: bfloat16 [4, 2048, 3, 1024], P('grp', 'tile'), may hold values from -6 to 6
- inst_weight: float32 [4], P('grp'), may hold values from 0.3 to 3
- filter_taps: bfloat16 [129], replicated, may hold values from 0.019897461 to 0.13964844
- basis_rows: bfloat16 [128, 16], replicated, may hold values from -0.5 to 0.5
- basis_cols: bfloat16 [128, 16], replicated, may hold values from -0.5 to 0.5
- box_table: int32 [128, 1], replicated, may hold values from 0 to 31
- owner_perm: int32 [32], replicated, may hold values from 0 to 31, each once
Outputs:
- design_grad: float32 [32, 3, 256], P(('grp', 'tile'))
Inputs may be any that keep to these rules, and one draw needn't show every extreme that they name: `box_table`: every one of the 32 boxes is named by at least one tile. `owner_perm`: each box appears exactly once.
All inputs are finite; a program needn't handle non-finite values.
Results may differ from a plain program's by a relative error of at most 0.017.
Values may be sent and summed in bfloat16 or wider, within the bound.
A program may use at most 64 MiB of HBM per device.

v0:
```python
import jax
import jax.numpy as jnp
from jax import lax
from jax.sharding import PartitionSpec as P


def band_matrix(filter_taps, inputs, outputs):
    reach = filter_taps.shape[0] - 1
    period = jnp.concatenate([filter_taps, jnp.zeros((inputs - reach,), filter_taps.dtype)])
    repeated = jnp.broadcast_to(period[None, :], (outputs, inputs + 1)).reshape(-1)
    return repeated[: outputs * inputs].reshape(outputs, inputs).T


def smooth_columns(field, filter_taps):
    reach = filter_taps.shape[0] - 1
    half = reach // 2
    width = field.shape[2]
    block = min(1024, width)
    padded = jnp.pad(field, ((0, 0), (0, 0), (half, half)))
    flat = padded.reshape(-1, width + reach)
    matrix = band_matrix(filter_taps, block + reach, block)
    pieces = jnp.dot(flat, matrix, preferred_element_type=jnp.float32)
    return pieces.reshape(field.shape).astype(jnp.bfloat16)


def smooth_rows_whole(field, filter_taps):
    reach = filter_taps.shape[0] - 1
    half = reach // 2
    height = field.shape[0]
    block = min(1024, height)
    padded = jnp.pad(field, ((half, half), (0, 0), (0, 0)))
    flat = padded.reshape(height + reach, -1)
    matrix = band_matrix(filter_taps, block + reach, block).T
    starts = jnp.arange(height // block, dtype=jnp.int32) * block

    def one_block(start):
        window = lax.dynamic_slice_in_dim(flat, start, block + reach, 0)
        return jnp.dot(matrix, window, preferred_element_type=jnp.float32)

    result = lax.map(one_block, starts)
    return result.reshape(field.shape).astype(jnp.bfloat16)


def contract_tiles(second, row_start, col_start, cols_all, basis_rows, basis_cols, box_table):
    local_rows = second.shape[0]
    local_cols = second.shape[2]
    tile_rows = basis_rows.shape[0]
    tile_cols = basis_cols.shape[0]
    ctrl_rows = basis_rows.shape[1]
    ctrl_cols = basis_cols.shape[1]
    row_tiles = local_rows // tile_rows
    shaped = second.reshape(row_tiles, tile_rows, 3, local_cols)
    rowwise = jnp.einsum("takc,ap->tkpc", shaped, basis_rows, preferred_element_type=jnp.float32)
    columns = col_start + jnp.arange(local_cols, dtype=jnp.int32)
    local_basis = basis_cols[columns % tile_cols].astype(jnp.float32)
    col_tiles = 1
    which_tile = jnp.zeros((local_cols,), jnp.int32)
    select = (which_tile[:, None] == jnp.arange(col_tiles, dtype=jnp.int32)[None, :]).astype(
        jnp.float32
    )
    spread = (local_basis[:, None, :] * select[:, :, None]).reshape(
        local_cols, col_tiles * ctrl_cols
    )
    tile_part = jnp.einsum("tkpc,cm->tkpm", rowwise, spread, precision=lax.Precision.HIGHEST)
    tile_part = tile_part.reshape(row_tiles, 3, ctrl_rows, col_tiles, ctrl_cols)
    tile_part = tile_part.transpose(0, 3, 1, 2, 4).reshape(
        row_tiles * col_tiles, 3 * ctrl_rows * ctrl_cols
    )
    tile_row_ids = row_start // tile_rows + jnp.arange(row_tiles, dtype=jnp.int32)
    tile_col_ids = col_start // tile_cols + jnp.arange(col_tiles, dtype=jnp.int32)
    tile_ids = (tile_row_ids[:, None] * (cols_all // tile_cols) + tile_col_ids[None, :]).reshape(-1)
    tile_boxes = box_table[tile_ids, 0]
    return (tile_part, tile_boxes)


def to_slots(tile_part, tile_boxes, slot_boxes):
    onehot = (tile_boxes[:, None] == slot_boxes[None, :]).astype(jnp.float32)
    return jnp.dot(onehot.T, tile_part, precision=lax.Precision.HIGHEST)


def local(sensitivity, inst_weight, filter_taps, basis_rows, basis_cols, box_table, owner_perm):
    cols_all = sensitivity.shape[3]
    ctrl_count = basis_rows.shape[1] * basis_cols.shape[1]
    summed = jnp.sum(
        sensitivity.astype(jnp.float32) * inst_weight[:, None, None, None], axis=0
    ).astype(jnp.bfloat16)
    first = smooth_columns(summed, filter_taps)
    strips = lax.all_to_all(first, "tile", split_axis=2, concat_axis=0, tiled=True)
    second = smooth_rows_whole(strips, filter_taps)
    col_start = lax.axis_index("tile") * strips.shape[2]
    tile_part, tile_boxes = contract_tiles(
        second, 0, col_start, cols_all, basis_rows, basis_cols, box_table
    )
    ordered = to_slots(tile_part, tile_boxes, owner_perm)
    owned = lax.psum_scatter(ordered, ("grp", "tile"), scatter_dimension=0, tiled=True)
    return owned.reshape(-1, 3, ctrl_count)


def solution(mesh):
    placed = (P("grp", "tile", None, None), P("grp"), P(), P(), P(), P(), P())
    return jax.shard_map(
        local, mesh=mesh, in_specs=placed, out_specs=P(("grp", "tile"), None, None), check_vma=False
    )
```

profile of v0, /device:TPU:0, one launch (start us, length us, event | category | flops | bytes accessed | tf_op | source)
XLA Modules:
  0.0 198.1 jit_solution(14179966924379345096)
XLA Ops:
  6.5 0.7 concatenate.8
  7.4 5.3 %reshape.101 = bf16[1180672]{0:T(1024)(128)(2,1)} reshape(bf16[1024,1153]{1,0:T(8,128)(2,1)S(1)} %broadcast_in_dim.8) | data formatting | bytes 4722688 | tf_op jit(solution)/shard_map/reshape | solution.py:10
  12.7 1.7 slice.9
  14.4 3.8 %reshape.119 = bf16[1024,1152,1]{1,0,2:T(8,128)(2,1)} reshape(bf16[1179648]{0:T(1024)(128)(2,1)S(1)} %slice.9) | data formatting | bytes 4718592 | tf_op jit(solution)/shard_map/reshape | solution.py:11
  18.2 2.0 %multiply_reduce_fusion = bf16[128,3,1024]{2,0,1:T(8,128)(2,1)S(1)} fusion(bf16[2,128,3,1024]{3,1,2,0:T(8,128)(2,1)} %param.9, f32[2]{0:T(128)S(1)} %copy-done.5), kind=kLoop, calls=%fused_computation.6 | loop fusion | flops 1966080 | bytes 2359304 | tf_op jit(solution)/shard_map/reduce_sum | solution.py:84
  20.4 1.2 convolution_convert_fusion
  21.6 1.4 copy.18
  23.0 7.4 %all-to-all-start = ((bf16[128,3,1024]{0,1,2:T(4,128)(2,1)}), bf16[128,3,1024]{0,1,2:T(4,128)(2,1)S(1)}, u32[]{:S(2)}, u32[]{:S(2)}) async-start(bf16[128,3,1024]{0,1,2:T(4,128)(2,1)} %copy.18), calls=%async_computation | async-start | bytes 2097152 | tf_op jit(solution)/shard_map/all_to_all | solution.py:88
  30.5 4.6 %reshape.102 = bf16[1024,1152]{1,0:T(8,128)(2,1)S(1)} reshape(bf16[1179648]{0:T(1024)(128)(2,1)} %copy-done.2) | data formatting | bytes 4718592 | tf_op jit(solution)/shard_map/reshape | solution.py:11
  35.3 0.7 gather_fusion
  36.0 0.6 gather_fusion.1
  36.6 16.7 %all-to-all-done = bf16[128,3,1024]{0,1,2:T(4,128)(2,1)S(1)} async-done(((bf16[128,3,1024]{0,1,2:T(4,128)(2,1)}), bf16[128,3,1024]{0,1,2:T(4,128)(2,1)S(1)}, u32[]{:S(2)}, u32[]{:S(2)}) %all-to-all-start) | async-done | bytes 786464 | tf_op jit(solution)/shard_map/all_to_all | solution.py:88
  54.0 8.3 %while.10 = (s32[]{:T(128)}, bf16[2,1024,192]{1,2,0:T(8,128)(2,1)}, s32[2]{0:T(128)S(1)}, bf16[2176,192]{0,1:T(8,128)(2,1)S(1)}, bf16[1024,1152]{1,0:T(8,128)(2,1)S(1)}, /*index=5*/s32[]{:T(128)}, s32[]{:T(128)}, s32[]{:T(128)}) while((s32[]{:T(128)}, bf16[2,1024,192]{1,2,0:T(8,128)(2,1)}, s32[2]{0:T(128)S(1)}, ...), condition=%wide.region_2.3_spmd, body=%wide.region_1.2_spmd.sunk | while | flops 452984832 | bytes 3588743 | solution.py:40
  54.0 0.6 dynamic_slice.12
  56.5 1.7 fusion.27
  58.2 0.6 dynamic_slice.12
  60.6 1.7 fusion.27
  62.3 1.9 copy.22
  64.3 0.5 convert_element_type.26
  64.8 0.7 convolution_bitcast_fusion.1
  65.5 0.3 fusion.5
  66.1 0.9 fusion.7
  67.0 122.9 %all-reduce.7.cloned.1.call-done = f32[32,768]{1,0:T(8,128)} async-done(((f32[32,768]{1,0:T(8,128)}), f32[32,768]{1,0:T(8,128)}) %all-reduce.7.cloned.1.call-update) | async-done | bytes 98320
  190.0 1.3 constant_dynamic-slice_fusion
  (27 shorter events, 1.4 us)
Async XLA Ops:
  6.5 58.3 %copy-start = (bf16[128,16]{0,1:T(8,128)(2,1)S(1)}, bf16[128,16]{0,1:T(8,128)(2,1)}, u32[]{:S(2)}) copy-start(bf16[128,16]{0,1:T(8,128)(2,1)} %param.12) | copy-start | bytes 12292
  14.4 5.8 %copy-start.2 = (bf16[1179648]{0:T(1024)(128)(2,1)}, bf16[1179648]{0:T(1024)(128)(2,1)S(1)}, u32[]{:S(2)}) copy-start(bf16[1179648]{0:T(1024)(128)(2,1)S(1)} %slice.9) | copy-start | bytes 7077892
  14.4 3.8 %copy-start.5 = (f32[2]{0:T(128)S(1)}, f32[2]{0:T(128)}, u32[]{:S(2)}) copy-start(f32[2]{0:T(128)} %param.10) | copy-start | bytes 28
  18.2 2.1 %copy-start.3 = (bf16[1024,1152,1]{1,0,2:T(8,128)(2,1)S(1)}, bf16[1024,1152,1]{1,0,2:T(8,128)(2,1)}, u32[]{:S(2)}) copy-start(bf16[1024,1152,1]{1,0,2:T(8,128)(2,1)} %reshape.119) | copy-start | bytes 7077892
  23.0 30.3 %all-to-all-start = ((bf16[128,3,1024]{0,1,2:T(4,128)(2,1)}), bf16[128,3,1024]{0,1,2:T(4,128)(2,1)S(1)}, u32[]{:S(2)}, u32[]{:S(2)}) async-start(bf16[128,3,1024]{0,1,2:T(4,128)(2,1)} %copy.18), calls=%async_computation | async-start | bytes 2097152 | tf_op jit(solution)/shard_map/all_to_all | solution.py:88
  30.4 159.5 %all-reduce.7.cloned.1.call-start = ((), (), s32[]{:S(2)}) async-start(), calls=%async_computation.1 | async-start | bytes 196608
  30.5 4.7 %copy-start.4 = (bf16[128,16]{0,1:T(8,128)(2,1)S(1)}, bf16[128,16]{0,1:T(8,128)(2,1)}, u32[]{:S(2)}) copy-start(bf16[128,16]{0,1:T(8,128)(2,1)} %param.13) | copy-start | bytes 12292
  30.5 4.8 %copy-start.1 = (s32[128,1]{0,1:T(1,128)S(1)}, s32[128,1]{0,1:T(1,128)}, u32[]{:S(2)}) copy-start(s32[128,1]{0,1:T(1,128)} %param.14) | copy-start | bytes 1540
  64.3 1.8 copy-start.6
Sparse Core Ops, SparseCore 0:
  67.1 122.7 all-reduce.6
where the time goes:
time: 199 us; the launch traced here: 198 us
  waiting for transfers between devices  140 us (70%)
  local copies, waits for them, and re-layouts  25.1 us (13%)
  between operations  13.6 us (7%)
  starting transfers between devices  7.4 us (4%)
  matrix products  6.66 us (3%)
  loops' own time  3.65 us (2%)
  other arithmetic  2.02 us (1%)
    unnamed x2, waiting for transfers between devices  123 us
    all_to_all x1, waiting for transfers between devices, local(): lax.all_to_all(first, 'tile', split_axis=2, concat_axis=0, tiled=True)  16.7 us
    reshape x2, local copies, waits for them, and re-layouts, band_matrix(): return repeated[:outputs * inputs].reshape(outputs, inputs).T  8.42 us
    all_to_all x1, starting transfers between devices, local(): lax.all_to_all(first, 'tile', split_axis=2, concat_axis=0, tiled=True)  7.36 us
    reshape x1, local copies, waits for them, and re-layouts, band_matrix(): jnp.broadcast_to(period[None, :], (outputs, inputs + 1)).reshape(-1)  5.3 us
  transfers between devices with their start and end apart: 2, of which 2 were waited for; matrix products, arithmetic and copies ran while one was open for 3% of the time, Pallas kernels for 0%

commit v1 on v0

v1 whole, which is shorter than its diff:
```python
import functools

import jax
import jax.numpy as jnp
from jax import lax
from jax.experimental import pallas as pl
from jax.experimental.pallas import tpu as pltpu
from jax.sharding import PartitionSpec as P

MESH = pl.DeviceIdType.MESH
F32 = jnp.float32
BF16 = jnp.bfloat16
LANES = 128


def iota(shape, dim):
    return lax.broadcasted_iota(jnp.int32, shape, dim)


def dot(a, b):
    return jnp.dot(a, b, preferred_element_type=F32)


def kernel(
    dims, sens_hbm, weight, taps_ref, rows_ref, cols_ref, table_ref, owner_ref, out_ref,
    sens, taps_wide, col_op, msg, recv, load_sem, send_sem, recv_sem,
):
    grps, tiles = dims
    devices = grps * tiles
    insts, comps, height, width = sens.shape
    ctrl, tile = rows_ref.shape
    tile_cols = width // tile
    half = (taps_ref.shape[1] - 1) // 2
    wide = 3 * tile
    low = LANES // ctrl
    high = ctrl // low
    slots = owner_ref.shape[1]
    ntiles = table_ref.shape[1]
    tile_pos = lax.axis_index("tile")
    me = lax.axis_index("grp") * tiles + tile_pos

    load = pltpu.make_async_copy(sens_hbm, sens, load_sem)
    load.start()

    barrier = pltpu.get_barrier_semaphore()

    def greet(step, carry):
        to = lax.rem(me + step, devices)
        pl.semaphore_signal(
            barrier, inc=1, device_id=(to // tiles, lax.rem(to, tiles)), device_id_type=MESH
        )
        return carry

    lax.fori_loop(1, devices, greet, 0)

    taps_wide[...] = jnp.zeros_like(taps_wide)
    taps_wide[:, : taps_ref.shape[1]] = taps_ref[...].astype(F32)
    spread = jnp.broadcast_to(taps_wide[...], (tile, wide))
    band = pltpu.roll(spread, tile - half, 1, stride=1, stride_axis=0).astype(BF16)
    row_op = dot(rows_ref[...], band).astype(BF16)
    piece = dot(cols_ref[...], band).astype(BF16)
    col_op[...] = jnp.zeros_like(col_op)
    for y in range(tile_cols):
        first = max(y - 1, 0)
        last = min(y + 2, tile_cols)
        col_op[y * ctrl : (y + 1) * ctrl, first * tile : last * tile] = piece[
            :, (first - y + 1) * tile : (last - y + 1) * tile
        ]
    row_ops = jnp.concatenate(
        [row_op[:, d * tile : (d + 1) * tile] for d in (2, 1, 0)], axis=0
    )

    owner_wide = jnp.broadcast_to(owner_ref[...].astype(F32), (slots, slots))
    owner = jnp.sum(
        jnp.where(iota((slots, slots), 0) == iota((slots, slots), 1), owner_wide, 0.0),
        axis=1, keepdims=True,
    )
    hit = jnp.where(owner == table_ref[...].astype(F32), 1.0, 0.0).astype(BF16)
    span = tile_cols * 3 * low
    lane = iota((ntiles, span), 1)
    y_of = lane // (3 * low)
    x_of = lax.rem(lane // low, 3) + tile_pos - 1
    wanted = (iota((ntiles, span), 0) == x_of * tile_cols + y_of) & (x_of >= 0) & (x_of < tiles)
    select = dot(hit, jnp.where(wanted, 1.0, 0.0).astype(BF16)).astype(BF16)

    copies = tile_cols * LANES
    from_row = iota((LANES, copies), 0)
    to_lane = iota((LANES, copies), 1)
    expand = jnp.where(
        (from_row // ctrl == to_lane // LANES) & (lax.rem(from_row, ctrl) == lax.rem(to_lane, ctrl)),
        1.0, 0.0,
    ).astype(BF16)
    keep = iota((low, LANES), 0) == iota((low, LANES), 1) // ctrl

    load.wait()
    field = sens[...].reshape(insts * comps * height, width)
    smooth = lax.dot_general(
        field, col_op[...], (((1,), (1,)), ((), ())), preferred_element_type=F32
    )
    block = comps * height
    total = weight[0] * smooth[:block]
    for i in range(1, insts):
        total = total + weight[i] * smooth[i * block : (i + 1) * block]
    total = total.astype(BF16)
    parts = jnp.concatenate(
        [dot(row_ops, total[k * height : (k + 1) * height]) for k in range(comps)], axis=0
    ).astype(BF16)
    grown = dot(parts, expand)
    columns = []
    for k in range(comps):
        for h in range(high):
            pieces = []
            for y in range(tile_cols):
                for d in range(3):
                    at = (k * 3 + d) * ctrl + h * low
                    pieces.append(
                        jnp.where(keep, grown[at : at + low, y * LANES : (y + 1) * LANES], 0.0)
                    )
            columns.append(jnp.concatenate(pieces, axis=0))
    stacked = jnp.concatenate(columns, axis=1).astype(BF16)
    boxes = dot(select, stacked)
    for j in range(comps * high):
        msg[:, j, :] = boxes[:, j * LANES : (j + 1) * LANES]

    pl.semaphore_wait(barrier, devices - 1)

    def push(step, carry):
        to = lax.rem(me + step, devices)
        pltpu.make_async_remote_copy(
            src_ref=msg.at[to],
            dst_ref=recv.at[step - 1],
            send_sem=send_sem,
            recv_sem=recv_sem,
            device_id=(to // tiles, lax.rem(to, tiles)),
            device_id_type=MESH,
        ).start()
        return carry

    lax.fori_loop(1, devices, push, 0)
    pltpu.make_async_copy(recv, recv, recv_sem).wait()
    result = msg[me] + jnp.sum(recv[...], axis=0)
    for k in range(comps):
        for h in range(high):
            j = k * high + h
            out_ref[0, k : k + 1, h * LANES : (h + 1) * LANES] = result[j : j + 1]
    pltpu.make_async_copy(recv, recv, send_sem).wait()


def solution(mesh):
    grps, tiles = mesh.shape["grp"], mesh.shape["tile"]
    devices = grps * tiles

    def local(sens, weight, taps, rows, cols, table, owner):
        field = sens.transpose(0, 2, 1, 3)
        insts, comps, height, width = field.shape
        tile, ctrl = rows.shape
        slots = owner.shape[0]
        assert height == tile and slots == devices and LANES % ctrl == 0
        assert width // tile * ctrl == LANES and ctrl * ctrl % LANES == 0
        vmem = pl.BlockSpec(memory_space=pltpu.VMEM)
        lines = comps * ctrl * ctrl // LANES
        return pl.pallas_call(
            functools.partial(kernel, (grps, tiles)),
            out_shape=jax.ShapeDtypeStruct((1, comps, ctrl * ctrl), F32),
            in_specs=[
                pl.BlockSpec(memory_space=pl.ANY),
                pl.BlockSpec(memory_space=pltpu.SMEM),
                vmem, vmem, vmem, vmem, vmem,
            ],
            out_specs=vmem,
            scratch_shapes=[
                pltpu.VMEM((insts, comps, height, width), BF16),
                pltpu.VMEM((1, 3 * tile), F32),
                pltpu.VMEM((LANES, width), BF16),
                pltpu.VMEM((slots, lines, LANES), F32),
                pltpu.VMEM((devices - 1, lines, LANES), F32),
                pltpu.SemaphoreType.DMA,
                pltpu.SemaphoreType.DMA,
                pltpu.SemaphoreType.DMA,
            ],
            compiler_params=pltpu.CompilerParams(
                collective_id=0, has_side_effects=True, vmem_limit_bytes=32 * 1024 * 1024
            ),
        )(
            field, weight, taps.reshape(1, -1), rows.T, cols.T,
            table.reshape(1, -1), owner.reshape(1, -1),
        )

    placed = (P("grp", "tile", None, None), P("grp"), P(), P(), P(), P(), P())
    return jax.shard_map(
        local, mesh=mesh, in_specs=placed, out_specs=P(("grp", "tile"), None, None), check_vma=False
    )
```

time: 199 us -> 17.7 us (0.09)
  waiting for transfers between devices: 140 us -> 0 us
  local copies, waits for them, and re-layouts: 25.1 us -> 5.98 us
  between operations: 13.6 us -> 0.02 us
  Pallas kernels: 0 us -> 11.4 us
  starting transfers between devices: 7.4 us -> 0 us
  matrix products: 6.66 us -> 0 us
  loops' own time: 3.65 us -> 0 us
  other arithmetic: 2.02 us -> 0 us
    unnamed x2 -> x0, waiting for transfers between devices: 123 us -> none
    all_to_all x1 -> x0, waiting for transfers between devices: 16.7 us -> none  [local(): lax.all_to_all(first, 'tile', split_axis=2, concat_axis=0, tiled=True)]
    reshape x3 -> x1, local copies, waits for them, and re-layouts: 13.7 us -> 0.66 us  [local(): taps.reshape(1, -1)]
    pallas_call x0 -> x1, Pallas kernels: none -> 11.4 us  [local(): pl.pallas_call(functools.partial(kernel, (grps, tiles)), out_shape=jax.Sh...]
    all_to_all x1 -> x0, starting transfers between devices: 7.36 us -> none  [local(): lax.all_to_all(first, 'tile', split_axis=2, concat_axis=0, tiled=True)]
    dot_general x6 -> x0, matrix products: 6.66 us -> none  [the longest x2 3.44 us: one_block(): return jnp.dot(matrix, window, preferred_element_type=jnp.float32)]
    convert_element_type x3 -> x0, local copies, waits for them, and re-layouts: 3.86 us -> none  [the longest x2 2.44 us: smooth_rows_whole(): return result.reshape(field.shape).astype(jnp.bfloat16)]
    another operation x1 -> x0, loops' own time: 3.65 us -> none  [smooth_rows_whole(): result = lax.map(one_block, starts)]
  transfers between devices with their start and end apart: 2 -> 0, of which waited for: 2 -> 0; matrix products, arithmetic and copies ran while one was open for 3% -> 0% of each run, Pallas kernels for 0% -> 0%
where the time goes in v1:
time: 17.7 us; the launch traced here: 17.4 us
  Pallas kernels  11.4 us (64%)
  local copies, waits for them, and re-layouts  5.98 us (34%)
    pallas_call x1, Pallas kernels, local(): pl.pallas_call(functools.partial(kernel, (grps, tiles)), out_shape=jax.Sh...  11.4 us
    unnamed x12, local copies, waits for them, and re-layouts  4.74 us
    reshape x1, local copies, waits for them, and re-layouts, local(): taps.reshape(1, -1)  0.66 us
    pallas_call x1, local copies, waits for them, and re-layouts, local(): pl.pallas_call(functools.partial(kernel, (grps, tiles)), out_shape=jax.Sh...  0.58 us

profile of v1, /device:TPU:0, one launch (start us, length us, event | category | flops | bytes accessed | tf_op | source)
XLA Modules:
  0.0 17.4 jit_solution(16581499876402939054)
XLA Ops:
  0.0 0.7 %reshape.9.taps_ref = bf16[1,129]{1,0:T(2,128)(2,1)S(1)} reshape(bf16[129]{0:T(256)(128)(2,1)} %param.9) | data formatting | bytes 516 | tf_op jit(solution)/shard_map/reshape | solution.py:185
  0.7 0.0 copy-start
  0.7 1.4 %copy-done = bf16[2,128,3,1024]{3,1,2,0:T(8,128)(2,1)S(1)} copy-done((bf16[2,128,3,1024]{3,1,2,0:T(8,128)(2,1)S(1)}, bf16[2,128,3,1024]{3,1,2,0:T(8,128)(2,1)}, u32[]{:S(2)}) %copy-start) | copy-done | bytes 1572888
  2.1 0.0 copy-start.1
  2.1 0.7 %copy-done.1 = bf16[128,16]{0,1:T(8,128)(2,1)S(1)} copy-done((bf16[128,16]{0,1:T(8,128)(2,1)S(1)}, bf16[128,16]{0,1:T(8,128)(2,1)}, u32[]{:S(2)}) %copy-start.1) | copy-done | bytes 4120
  2.8 0.0 copy-start.2
  2.8 0.7 %copy-done.2 = bf16[128,16]{0,1:T(8,128)(2,1)S(1)} copy-done((bf16[128,16]{0,1:T(8,128)(2,1)S(1)}, bf16[128,16]{0,1:T(8,128)(2,1)}, u32[]{:S(2)}) %copy-start.2) | copy-done | bytes 4120
  3.4 0.0 copy-start.3
  3.4 0.7 %copy-done.3 = f32[2]{0:T(128)S(1)} copy-done((f32[2]{0:T(128)S(1)}, f32[2]{0:T(128)}, u32[]{:S(2)}) %copy-start.3) | copy-done | bytes 32
  4.1 0.0 copy-start.4
  4.1 0.7 %copy-done.4 = s32[128,1]{0,1:T(1,128)S(1)} copy-done((s32[128,1]{0,1:T(1,128)S(1)}, s32[128,1]{0,1:T(1,128)}, u32[]{:S(2)}) %copy-start.4) | copy-done | bytes 536
  4.8 0.0 copy-start.5
  4.8 0.7 %copy-done.5 = s32[32]{0:T(128)S(1)} copy-done((s32[32]{0:T(128)S(1)}, s32[32]{0:T(128)}, u32[]{:S(2)}) %copy-start.5) | copy-done | bytes 152
  5.4 11.4 %shard_map.73 = f32[1,3,256]{2,1,0:T(4,128)S(1)} custom-call(bf16[2,3,128,1024]{3,2,1,0:T(8,128)(2,1)S(1)} %bitcast.5, f32[2]{0:T(128)S(1)} %copy-done.3, bf16[1,129]{1,0:T(2,128)(2,1)S(1)} %reshape.9.taps_ref, bf16[16,128]{1,0:T(8,128)(2,1)S(1)} %bitcast.6, bf16[16,128]{1,0:T(8,128)(2,1)S(1)} %bitcast.7, s32[1,128]{1,0:T(1,128)S(1)} %bitcast.8, ...), custom_call_target="tpu_custom_call" | custom-call | tf_op jit(solution)/shard_map/pallas_call | solution.py:162
  16.9 0.6 %copy.8 = f32[1,3,256]{2,0,1:T(1,128)} copy(f32[1,3,256]{2,1,0:T(4,128)S(1)} %shard_map.73) | data formatting | bytes 6144 | tf_op jit(solution)/shard_map/pallas_call | solution.py:162
Async XLA Ops:
  0.7 1.4 %copy-start = (bf16[2,128,3,1024]{3,1,2,0:T(8,128)(2,1)S(1)}, bf16[2,128,3,1024]{3,1,2,0:T(8,128)(2,1)}, u32[]{:S(2)}) copy-start(bf16[2,128,3,1024]{3,1,2,0:T(8,128)(2,1)} %param.7) | copy-start | bytes 4718596
  2.1 0.7 %copy-start.1 = (bf16[128,16]{0,1:T(8,128)(2,1)S(1)}, bf16[128,16]{0,1:T(8,128)(2,1)}, u32[]{:S(2)}) copy-start(bf16[128,16]{0,1:T(8,128)(2,1)} %param.10) | copy-start | bytes 12292
  2.8 0.7 %copy-start.2 = (bf16[128,16]{0,1:T(8,128)(2,1)S(1)}, bf16[128,16]{0,1:T(8,128)(2,1)}, u32[]{:S(2)}) copy-start(bf16[128,16]{0,1:T(8,128)(2,1)} %param.11) | copy-start | bytes 12292
  3.4 0.7 %copy-start.3 = (f32[2]{0:T(128)S(1)}, f32[2]{0:T(128)}, u32[]{:S(2)}) copy-start(f32[2]{0:T(128)} %weight.1) | copy-start | bytes 28
  4.1 0.7 %copy-start.4 = (s32[128,1]{0,1:T(1,128)S(1)}, s32[128,1]{0,1:T(1,128)}, u32[]{:S(2)}) copy-start(s32[128,1]{0,1:T(1,128)} %param.12) | copy-start | bytes 1540
  4.8 0.7 %copy-start.5 = (s32[32]{0:T(128)S(1)}, s32[32]{0:T(128)}, u32[]{:S(2)}) copy-start(s32[32]{0:T(128)} %param.13) | copy-start | bytes 388

commit v2 on v1

--- a/solution.py
+++ b/solution.py
@@ -22,15 +22,16 @@
 
 
 def kernel(
-    dims, sens_hbm, weight, taps_ref, rows_ref, cols_ref, table_ref, owner_ref, out_ref,
-    sens, taps_wide, col_op, msg, recv, load_sem, send_sem, recv_sem,
+    dims, sens_hbm, weight_hbm, taps_hbm, rows_hbm, cols_hbm, table_hbm, owner_hbm, out_ref,
+    sens, weight, taps_ref, rows_ref, cols_ref, table_ref, owner_ref,
+    taps_wide, col_op, msg, recv, load_sems, send_sem, recv_sem,
 ):
     grps, tiles = dims
     devices = grps * tiles
     insts, comps, height, width = sens.shape
     ctrl, tile = rows_ref.shape
     tile_cols = width // tile
-    half = (taps_ref.shape[1] - 1) // 2
+    half = (taps_ref.shape[0] - 1) // 2
     wide = 3 * tile
     low = LANES // ctrl
     high = ctrl // low
@@ -39,8 +40,16 @@
     tile_pos = lax.axis_index("tile")
     me = lax.axis_index("grp") * tiles + tile_pos
 
-    load = pltpu.make_async_copy(sens_hbm, sens, load_sem)
-    load.start()
+    loads = [
+        pltpu.make_async_copy(source, held, load_sems.at[n])
+        for n, (source, held) in enumerate((
+            (taps_hbm, taps_ref), (rows_hbm, rows_ref), (cols_hbm, cols_ref),
+            (owner_hbm, owner_ref), (table_hbm, table_ref), (weight_hbm, weight),
+            (sens_hbm, sens),
+        ))
+    ]
+    for load in loads:
+        load.start()
 
     barrier = pltpu.get_barrier_semaphore()
 
@@ -54,7 +63,9 @@
     lax.fori_loop(1, devices, greet, 0)
 
     taps_wide[...] = jnp.zeros_like(taps_wide)
-    taps_wide[:, : taps_ref.shape[1]] = taps_ref[...].astype(F32)
+    for load in loads[:-1]:
+        load.wait()
+    taps_wide[:, : taps_ref.shape[0]] = taps_ref[...].astype(F32).reshape(1, -1)
     spread = jnp.broadcast_to(taps_wide[...], (tile, wide))
     band = pltpu.roll(spread, tile - half, 1, stride=1, stride_axis=0).astype(BF16)
     row_op = dot(rows_ref[...], band).astype(BF16)
@@ -92,7 +103,7 @@
     ).astype(BF16)
     keep = iota((low, LANES), 0) == iota((low, LANES), 1) // ctrl
 
-    load.wait()
+    loads[-1].wait()
     field = sens[...].reshape(insts * comps * height, width)
     smooth = lax.dot_general(
         field, col_op[...], (((1,), (1,)), ((), ())), preferred_element_type=F32
@@ -142,7 +153,7 @@
     for k in range(comps):
         for h in range(high):
             j = k * high + h
-            out_ref[0, k : k + 1, h * LANES : (h + 1) * LANES] = result[j : j + 1]
+            out_ref[k, :, h * LANES : (h + 1) * LANES] = result[j : j + 1]
     pltpu.make_async_copy(recv, recv, send_sem).wait()
 
 
@@ -157,34 +168,34 @@
         slots = owner.shape[0]
         assert height == tile and slots == devices and LANES % ctrl == 0
         assert width // tile * ctrl == LANES and ctrl * ctrl % LANES == 0
-        vmem = pl.BlockSpec(memory_space=pltpu.VMEM)
         lines = comps * ctrl * ctrl // LANES
         return pl.pallas_call(
             functools.partial(kernel, (grps, tiles)),
-            out_shape=jax.ShapeDtypeStruct((1, comps, ctrl * ctrl), F32),
-            in_specs=[
-                pl.BlockSpec(memory_space=pl.ANY),
-                pl.BlockSpec(memory_space=pltpu.SMEM),
-                vmem, vmem, vmem, vmem, vmem,
-            ],
-            out_specs=vmem,
+            out_shape=jax.ShapeDtypeStruct((comps, 1, ctrl * ctrl), F32),
+            in_specs=[pl.BlockSpec(memory_space=pltpu.HBM)] * 7,
+            out_specs=pl.BlockSpec(memory_space=pltpu.VMEM),
             scratch_shapes=[
                 pltpu.VMEM((insts, comps, height, width), BF16),
+                pltpu.SMEM(weight.shape, F32),
+                pltpu.VMEM(taps.shape, BF16),
+                pltpu.VMEM((ctrl, tile), BF16),
+                pltpu.VMEM((ctrl, tile), BF16),
+                pltpu.VMEM((1, table.shape[0]), jnp.int32),
+                pltpu.VMEM((1, slots), jnp.int32),
                 pltpu.VMEM((1, 3 * tile), F32),
                 pltpu.VMEM((LANES, width), BF16),
                 pltpu.VMEM((slots, lines, LANES), F32),
                 pltpu.VMEM((devices - 1, lines, LANES), F32),
-                pltpu.SemaphoreType.DMA,
+                pltpu.SemaphoreType.DMA((7,)),
                 pltpu.SemaphoreType.DMA,
                 pltpu.SemaphoreType.DMA,
             ],
             compiler_params=pltpu.CompilerParams(
-                collective_id=0, has_side_effects=True, vmem_limit_bytes=32 * 1024 * 1024
+                collective_id=0, has_side_effects=True
             ),
         )(
-            field, weight, taps.reshape(1, -1), rows.T, cols.T,
-            table.reshape(1, -1), owner.reshape(1, -1),
-        )
+            field, weight, taps, rows.T, cols.T, table.reshape(1, -1), owner.reshape(1, -1)
+        ).transpose(1, 0, 2)
 
     placed = (P("grp", "tile", None, None), P("grp"), P(), P(), P(), P(), P())
     return jax.shard_map(

time: 17.7 us -> 13.4 us (0.76)
  local copies, waits for them, and re-layouts: 5.98 us -> 1.26 us
  Pallas kernels: 11.4 us -> 12 us
    unnamed x12 -> x1, local copies, waits for them, and re-layouts: 4.74 us -> 1.26 us
    reshape x1 -> x0, local copies, waits for them, and re-layouts: 0.66 us -> none  [local(): taps.reshape(1, -1)]
    pallas_call x1 -> x0, local copies, waits for them, and re-layouts: 0.58 us -> none  [local(): pl.pallas_call(functools.partial(kernel, (grps, tiles)), out_shape=jax.Sh...]
    pallas_call x1, Pallas kernels: 11.4 us -> 12 us  [local(): pl.pallas_call(functools.partial(kernel, (grps, tiles)), out_shape=jax.Sh...]
where the time goes in v2:
time: 13.4 us; the launch traced here: 13.2 us
  Pallas kernels  12 us (90%)
  local copies, waits for them, and re-layouts  1.26 us (9%)
    pallas_call x1, Pallas kernels, local(): pl.pallas_call(functools.partial(kernel, (grps, tiles)), out_shape=jax.Sh...  12 us
    unnamed x1, local copies, waits for them, and re-layouts  1.26 us

profile of v2, /device:TPU:0, one launch (start us, length us, event | category | flops | bytes accessed | tf_op | source)
XLA Modules:
  0.0 13.2 jit_solution(17277985078448448731)
XLA Ops:
  0.0 12.0 %shard_map.73 = f32[3,1,256]{2,1,0:T(1,128)} custom-call(bf16[2,3,128,1024]{3,2,1,0:T(8,128)(2,1)} %bitcast.6, f32[2]{0:T(128)} %weight_hbm.1, bf16[129]{0:T(256)(128)(2,1)} %taps_hbm.1, bf16[16,128]{1,0:T(8,128)(2,1)} %bitcast.8, bf16[16,128]{1,0:T(8,128)(2,1)} %bitcast.9, s32[1,128]{1,0:T(1,128)} %bitcast.10, s32[1,32]{1,0:T(1,128)} %bitcast.11), custom_call_target="tpu_custom_call" | custom-call | tf_op jit(solution)/shard_map/pallas_call | solution.py:172
  12.0 1.3 %copy.9 = f32[1,3,256]{2,0,1:T(1,128)} copy(f32[1,3,256]{2,0,1:T(1,128)} %bitcast.7) | data formatting | bytes 6144

commit v3 on v2

--- a/solution.py
+++ b/solution.py
@@ -24,7 +24,7 @@
 def kernel(
     dims, sens_hbm, weight_hbm, taps_hbm, rows_hbm, cols_hbm, table_hbm, owner_hbm, out_ref,
     sens, weight, taps_ref, rows_ref, cols_ref, table_ref, owner_ref,
-    taps_wide, col_op, msg, recv, load_sems, send_sem, recv_sem,
+    taps_wide, col_op, wanted_ref, expand_ref, msg, recv, load_sems, send_sem, recv_sem,
 ):
     grps, tiles = dims
     devices = grps * tiles
@@ -63,14 +63,29 @@
     lax.fori_loop(1, devices, greet, 0)
 
     taps_wide[...] = jnp.zeros_like(taps_wide)
-    for load in loads[:-1]:
+    col_op[...] = jnp.zeros_like(col_op)
+    span = tile_cols * 3 * low
+    lane = iota((ntiles, span), 1)
+    y_of = lane // (3 * low)
+    x_of = lax.rem(lane // low, 3) + tile_pos - 1
+    wanted = (iota((ntiles, span), 0) == x_of * tile_cols + y_of) & (x_of >= 0) & (x_of < tiles)
+    wanted_ref[...] = jnp.where(wanted, 1.0, 0.0).astype(BF16)
+    copies = tile_cols * LANES
+    from_row = iota((LANES, copies), 0)
+    to_lane = iota((LANES, copies), 1)
+    expand_ref[...] = jnp.where(
+        (from_row // ctrl == to_lane // LANES) & (lax.rem(from_row, ctrl) == lax.rem(to_lane, ctrl)),
+        1.0, 0.0,
+    ).astype(BF16)
+    keep = iota((low, LANES), 0) == iota((low, LANES), 1) // ctrl
+
+    for load in loads[:3]:
         load.wait()
     taps_wide[:, : taps_ref.shape[0]] = taps_ref[...].astype(F32).reshape(1, -1)
     spread = jnp.broadcast_to(taps_wide[...], (tile, wide))
     band = pltpu.roll(spread, tile - half, 1, stride=1, stride_axis=0).astype(BF16)
-    row_op = dot(rows_ref[...], band).astype(BF16)
-    piece = dot(cols_ref[...], band).astype(BF16)
-    col_op[...] = jnp.zeros_like(col_op)
+    both = dot(jnp.concatenate([rows_ref[...], cols_ref[...]], axis=0), band).astype(BF16)
+    row_op, piece = both[:ctrl], both[ctrl:]
     for y in range(tile_cols):
         first = max(y - 1, 0)
         last = min(y + 2, tile_cols)
@@ -81,29 +96,16 @@
         [row_op[:, d * tile : (d + 1) * tile] for d in (2, 1, 0)], axis=0
     )
 
+    for load in loads[3:]:
+        load.wait()
     owner_wide = jnp.broadcast_to(owner_ref[...].astype(F32), (slots, slots))
     owner = jnp.sum(
         jnp.where(iota((slots, slots), 0) == iota((slots, slots), 1), owner_wide, 0.0),
         axis=1, keepdims=True,
     )
     hit = jnp.where(owner == table_ref[...].astype(F32), 1.0, 0.0).astype(BF16)
-    span = tile_cols * 3 * low
-    lane = iota((ntiles, span), 1)
-    y_of = lane // (3 * low)
-    x_of = lax.rem(lane // low, 3) + tile_pos - 1
-    wanted = (iota((ntiles, span), 0) == x_of * tile_cols + y_of) & (x_of >= 0) & (x_of < tiles)
-    select = dot(hit, jnp.where(wanted, 1.0, 0.0).astype(BF16)).astype(BF16)
-
-    copies = tile_cols * LANES
-    from_row = iota((LANES, copies), 0)
-    to_lane = iota((LANES, copies), 1)
-    expand = jnp.where(
-        (from_row // ctrl == to_lane // LANES) & (lax.rem(from_row, ctrl) == lax.rem(to_lane, ctrl)),
-        1.0, 0.0,
-    ).astype(BF16)
-    keep = iota((low, LANES), 0) == iota((low, LANES), 1) // ctrl
-
-    loads[-1].wait()
+    select = dot(hit, wanted_ref[...]).astype(BF16)
+
     field = sens[...].reshape(insts * comps * height, width)
     smooth = lax.dot_general(
         field, col_op[...], (((1,), (1,)), ((), ())), preferred_element_type=F32
@@ -116,7 +118,7 @@
     parts = jnp.concatenate(
         [dot(row_ops, total[k * height : (k + 1) * height]) for k in range(comps)], axis=0
     ).astype(BF16)
-    grown = dot(parts, expand)
+    grown = dot(parts, expand_ref[...])
     columns = []
     for k in range(comps):
         for h in range(high):
@@ -135,26 +137,30 @@
 
     pl.semaphore_wait(barrier, devices - 1)
 
-    def push(step, carry):
-        to = lax.rem(me + step, devices)
-        pltpu.make_async_remote_copy(
-            src_ref=msg.at[to],
-            dst_ref=recv.at[step - 1],
-            send_sem=send_sem,
-            recv_sem=recv_sem,
-            device_id=(to // tiles, lax.rem(to, tiles)),
-            device_id_type=MESH,
-        ).start()
+    def push(to, carry):
+        @pl.when(to != me)
+        def _():
+            pltpu.make_async_remote_copy(
+                src_ref=msg.at[to],
+                dst_ref=recv.at[me],
+                send_sem=send_sem,
+                recv_sem=recv_sem,
+                device_id=(to // tiles, lax.rem(to, tiles)),
+                device_id_type=MESH,
+            ).start()
+
         return carry
 
-    lax.fori_loop(1, devices, push, 0)
-    pltpu.make_async_copy(recv, recv, recv_sem).wait()
-    result = msg[me] + jnp.sum(recv[...], axis=0)
+    lax.fori_loop(0, devices, push, 0)
+    recv[me] = msg[me]
+    others = recv.at[pl.ds(0, devices - 1)]
+    pltpu.make_async_copy(others, others, recv_sem).wait()
+    result = jnp.sum(recv[...], axis=0)
     for k in range(comps):
         for h in range(high):
             j = k * high + h
-            out_ref[k, :, h * LANES : (h + 1) * LANES] = result[j : j + 1]
-    pltpu.make_async_copy(recv, recv, send_sem).wait()
+            out_ref[0, k : k + 1, h * LANES : (h + 1) * LANES] = result[j : j + 1]
+    pltpu.make_async_copy(others, others, send_sem).wait()
 
 
 def solution(mesh):
@@ -171,7 +177,7 @@
         lines = comps * ctrl * ctrl // LANES
         return pl.pallas_call(
             functools.partial(kernel, (grps, tiles)),
-            out_shape=jax.ShapeDtypeStruct((comps, 1, ctrl * ctrl), F32),
+            out_shape=jax.ShapeDtypeStruct((1, comps, ctrl * ctrl), F32),
             in_specs=[pl.BlockSpec(memory_space=pltpu.HBM)] * 7,
             out_specs=pl.BlockSpec(memory_space=pltpu.VMEM),
             scratch_shapes=[
@@ -184,18 +190,25 @@
                 pltpu.VMEM((1, slots), jnp.int32),
                 pltpu.VMEM((1, 3 * tile), F32),
                 pltpu.VMEM((LANES, width), BF16),
+                pltpu.VMEM((table.shape[0], width // tile * 3 * (LANES // ctrl)), BF16),
+                pltpu.VMEM((LANES, width // tile * LANES), BF16),
                 pltpu.VMEM((slots, lines, LANES), F32),
-                pltpu.VMEM((devices - 1, lines, LANES), F32),
+                pltpu.VMEM((devices, lines, LANES), F32),
                 pltpu.SemaphoreType.DMA((7,)),
                 pltpu.SemaphoreType.DMA,
                 pltpu.SemaphoreType.DMA,
             ],
             compiler_params=pltpu.CompilerParams(
-                collective_id=0, has_side_effects=True
+                collective_id=0, has_side_effects=True, vmem_limit_bytes=32 * 1024 * 1024
             ),
         )(
-            field, weight, taps, rows.T, cols.T, table.reshape(1, -1), owner.reshape(1, -1)
-        ).transpose(1, 0, 2)
+            *(
+                pltpu.with_memory_space_constraint(operand, pltpu.HBM)
+                for operand in (
+                    field, weight, taps, rows.T, cols.T, table.reshape(1, -1), owner.reshape(1, -1)
+                )
+            )
+        )
 
     placed = (P("grp", "tile", None, None), P("grp"), P(), P(), P(), P(), P())
     return jax.shard_map(

time: 13.4 us -> 12.1 us (0.903)
  Pallas kernels: 12 us -> 11.3 us
  local copies, waits for them, and re-layouts: 1.26 us -> 0.58 us
    unnamed x1 -> x0, local copies, waits for them, and re-layouts: 1.26 us -> none
    pallas_call x1, Pallas kernels: 12 us -> 11.3 us  [local(): pl.pallas_call(functools.partial(kernel, (grps, tiles)), out_shape=jax.Sh...]
    pallas_call x0 -> x1, local copies, waits for them, and re-layouts: none -> 0.58 us  [local(): pl.pallas_call(functools.partial(kernel, (grps, tiles)), out_shape=jax.Sh...]
where the time goes in v3:
time: 12.1 us; the launch traced here: 11.9 us
  Pallas kernels  11.3 us (93%)
  local copies, waits for them, and re-layouts  0.58 us (5%)
    pallas_call x1, Pallas kernels, local(): pl.pallas_call(functools.partial(kernel, (grps, tiles)), out_shape=jax.Sh...  11.3 us
    pallas_call x1, local copies, waits for them, and re-layouts, local(): pl.pallas_call(functools.partial(kernel, (grps, tiles)), out_shape=jax.Sh...  0.58 us

profile of v3, /device:TPU:0, one launch (start us, length us, event | category | flops | bytes accessed | tf_op | source)
XLA Modules:
  0.0 11.9 jit_solution(3817701030358157322)
XLA Ops:
  0.0 11.3 %shard_map.73 = f32[1,3,256]{2,1,0:T(4,128)S(1)} custom-call(bf16[2,3,128,1024]{3,2,1,0:T(8,128)(2,1)} %bitcast.5, f32[2]{0:T(128)} %weight_hbm.1, bf16[129]{0:T(256)(128)(2,1)} %taps_hbm.1, bf16[16,128]{1,0:T(8,128)(2,1)} %bitcast.6, bf16[16,128]{1,0:T(8,128)(2,1)} %bitcast.7, s32[1,128]{1,0:T(1,128)} %bitcast.8, s32[1,32]{1,0:T(1,128)} %bitcast.9), custom_call_target="tpu_custom_call" | custom-call | tf_op jit(solution)/shard_map/pallas_call | solution.py:178
  11.3 0.6 %copy.8 = f32[1,3,256]{2,0,1:T(1,128)} copy(f32[1,3,256]{2,1,0:T(4,128)S(1)} %shard_map.73) | data formatting | bytes 6144 | tf_op jit(solution)/shard_map/pallas_call | solution.py:178
